TPU v7x, 32 devices: a whole 2x2x4 slice. The times are simulated.
32 devices in a mesh: batch: 16 (over z, y, core), seq: 2 (over x).
Axes of the slice: x: 2, y: 2, z: 4, core: 2. Of those that a mesh axis runs over, the one named last changes fastest.
Arguments:
- tokens: bfloat16 [48, 1024, 1024], P('batch', 'seq'), may hold values from -6 to 6
- cotangent: bfloat16 [48, 1024, 1024], P('batch', 'seq'), may hold values from -6 to 6
- layout: int32 [4], replicated, may hold values from 0 to 3, each once
- attention_norm_gain: float32 [1024], replicated, may hold values from 0.1 to 1.9
- feedforward_norm_gain: float32 [1024], replicated, may hold values from 0.1 to 1.9
- query_weight: bfloat16 [1024, 1024], P('batch'), may hold values from -0.25 to 0.25
- key_weight: bfloat16 [1024, 1024], P('batch'), may hold values from -0.25 to 0.25
- value_weight: bfloat16 [1024, 1024], P('batch'), may hold values from -0.1875 to 0.1875
- attention_output_weight: bfloat16 [1024, 1024], P('batch'), may hold values from -0.5 to 0.5
- up_weight: bfloat16 [1024, 4096], P('batch'), may hold values from -0.1875 to 0.1875
- down_weight: bfloat16 [4096, 1024], P('batch'), may hold values from -0.09375 to 0.09375
- query_down_adapter: bfloat16 [1024, 4], replicated, may hold values from -0.1875 to 0.1875
- query_up_adapter: bfloat16 [4, 1024], replicated, may hold values from -0.1796875 to 0.1796875
- value_down_adapter: bfloat16 [1024, 4], replicated, may hold values from -0.1875 to 0.1875
- value_up_adapter: bfloat16 [4, 1024], replicated, may hold values from -0.1796875 to 0.1796875
Outputs:
- layer_out: bfloat16 [48, 1024, 1024], P('batch', 'seq')
- input_grad: bfloat16 [48, 1024, 1024], P('batch', 'seq')
- grad_qa: float32 [1024, 4], replicated
- query_up_gradient: float32 [4, 1024], replicated
- grad_va: float32 [1024, 4], replicated
- value_up_gradient: float32 [4, 1024], replicated
Inputs may be any that keep to these rules, and one draw needn't show every extreme that they name: `layout`: a permutation: each position block of a document is held by exactly one stored block, the same for all documents.
All inputs are finite; a program needn't handle non-finite values.
Results may differ from a plain program's by a relative error of at most 0.018.
Values may be sent and summed in bfloat16 or wider, within the bound.
A program may use at most 384 MiB of HBM per device.

v0:
```python
import jax
import jax.numpy as jnp
from jax import lax
from jax.sharding import PartitionSpec as P

HEADS = 16
HEAD_DIM = 64


EPSILON = 1e-05
ADAPTER_SCALE = 8.0
SCORE_SCALE = 0.125
NEG_FILL = -1e30
GELU_C = 0.7978845608028654


def matrix_product(left_op, right_op):
    return jnp.dot(left_op, right_op, preferred_element_type=jnp.float32)


def contracted_against(left_op, right_op):
    return lax.dot_general(
        left_op, right_op, (((1,), (1,)), ((), ())), preferred_element_type=jnp.float32
    )


def across_documents(left_op, right_op):
    return lax.dot_general(
        left_op, right_op, (((0,), (0,)), ((), ())), preferred_element_type=jnp.float32
    )


def block_positions(layout, offset, rows_in, half_len):
    stored = offset + jnp.arange(rows_in, dtype=jnp.int32)
    matches = (stored // half_len)[:, None] == jnp.arange(layout.shape[0], dtype=jnp.int32)[None, :]
    return jnp.sum(jnp.where(matches, layout[None, :], 0), axis=1) * half_len + stored % half_len


def norm_fwd(values, gain_vec):
    row_mean = jnp.mean(values, axis=-1, keepdims=True)
    centred = values - row_mean
    spread = jnp.mean(centred * centred, axis=-1, keepdims=True)
    inverse = lax.rsqrt(spread + EPSILON)
    scaled = centred * inverse
    return (scaled * gain_vec, scaled, inverse)


def norm_back(values, gain_vec, upstream):
    unused_out, scaled, inverse = norm_fwd(values, gain_vec)
    inner_grad = upstream * gain_vec
    return inverse * (
        inner_grad
        - jnp.mean(inner_grad, axis=-1, keepdims=True)
        - scaled * jnp.mean(inner_grad * scaled, axis=-1, keepdims=True)
    )


def gelu_parts(pre_act):
    cubic = 0.044715 * pre_act * pre_act
    tanh_val = jnp.tanh(GELU_C * (pre_act + cubic * pre_act))
    gelu_value = 0.5 * pre_act * (1.0 + tanh_val)
    gelu_slope = 0.5 * (1.0 + tanh_val) + 0.5 * pre_act * (1.0 - tanh_val * tanh_val) * GELU_C * (
        1.0 + 3.0 * cubic
    )
    return (gelu_value, gelu_slope)


def masked_scores(query_heads, query_pos, key_heads, key_pos):
    scores = (
        jnp.einsum("qhd,khd->qhk", query_heads, key_heads, preferred_element_type=jnp.float32)
        * SCORE_SCALE
    )
    return jnp.where(key_pos[None, None, :] <= query_pos[:, None, None], scores, NEG_FILL)


def attend_fold(query_heads, query_pos, layout, half_len):

    def key_fold(state_in, segment, offset):
        run_max, run_sum, run_acc = state_in
        key_piece, value_piece = segment
        rows_in = key_piece.shape[0]
        key_heads = key_piece.reshape(rows_in, HEADS, HEAD_DIM)
        value_heads = value_piece.reshape(rows_in, HEADS, HEAD_DIM)
        key_pos = block_positions(layout, offset, rows_in, half_len)
        scores = masked_scores(query_heads, query_pos, key_heads, key_pos)
        new_max = jnp.maximum(run_max, jnp.max(scores, axis=-1))
        weights_now = jnp.exp(scores - new_max[..., None])
        new_sum = jnp.sum(weights_now, axis=-1)
        new_acc = jnp.einsum(
            "qhk,khd->qhd",
            weights_now.astype(jnp.bfloat16),
            value_heads,
            preferred_element_type=jnp.float32,
        )
        return (new_max, new_sum, new_acc)

    return key_fold


def grad_fold(query_heads, query_pos, grad_heads, log_total, row_delta, layout, half_len):

    def key_fold(state_in, segment, offset):
        key_piece, value_piece = segment
        rows_in = key_piece.shape[0]
        key_heads = key_piece.reshape(rows_in, HEADS, HEAD_DIM)
        value_heads = value_piece.reshape(rows_in, HEADS, HEAD_DIM)
        key_pos = block_positions(layout, offset, rows_in, half_len)
        scores = masked_scores(query_heads, query_pos, key_heads, key_pos)
        chances = jnp.exp(scores - log_total[..., None])
        chance_grad = jnp.einsum(
            "qhd,khd->qhk", grad_heads, value_heads, preferred_element_type=jnp.float32
        )
        score_grad = (chances * (chance_grad - row_delta[..., None])).astype(jnp.bfloat16)
        grad_query = SCORE_SCALE * jnp.einsum(
            "qhk,khd->qhd", score_grad, key_heads, preferred_element_type=jnp.float32
        )
        value_term = jnp.einsum(
            "qhk,qhd->khd",
            chances.astype(jnp.bfloat16),
            grad_heads,
            preferred_element_type=jnp.float32,
        )
        key_term = SCORE_SCALE * jnp.einsum(
            "qhk,qhd->khd", score_grad, query_heads, preferred_element_type=jnp.float32
        )
        key_part = key_term.reshape(rows_in, HEADS * HEAD_DIM)
        value_part = value_term.reshape(rows_in, HEADS * HEAD_DIM)
        return (grad_query, key_part, value_part)

    return key_fold


def local(
    tokens,
    cotangent,
    layout,
    attention_norm_gain,
    feedforward_norm_gain,
    query_weight,
    key_weight,
    value_weight,
    attention_output_weight,
    up_weight,
    down_weight,
    query_down_adapter,
    query_up_adapter,
    value_down_adapter,
    value_up_adapter,
):
    frozen_full = (
        lax.all_gather(query_weight, "batch", axis=0, tiled=True),
        lax.all_gather(key_weight, "batch", axis=0, tiled=True),
        lax.all_gather(value_weight, "batch", axis=0, tiled=True),
        lax.all_gather(attention_output_weight, "batch", axis=0, tiled=True),
        lax.all_gather(up_weight, "batch", axis=0, tiled=True),
        lax.all_gather(down_weight, "batch", axis=0, tiled=True),
    )
    local_len = tokens.shape[1]
    model_width = tokens.shape[2]
    seq_ways = lax.axis_size("seq")
    total_len = local_len * seq_ways
    half_len = local_len // 2
    local_start = lax.axis_index("seq") * local_len
    query_pos = block_positions(layout, local_start, local_len, half_len)

    def forward_one(unused, token_block):
        complete_query, full_k, complete_value, full_o, full_up, full_down = frozen_full
        inputs = token_block.astype(jnp.float32)
        normed, unused_scaled, unused_inv = norm_fwd(inputs, attention_norm_gain)
        first_normalized = normed.astype(jnp.bfloat16)
        reduced_query = matrix_product(first_normalized, query_down_adapter).astype(jnp.bfloat16)
        reduced_value = matrix_product(first_normalized, value_down_adapter).astype(jnp.bfloat16)
        query_rows = (
            matrix_product(first_normalized, complete_query)
            + ADAPTER_SCALE * matrix_product(reduced_query, query_up_adapter)
        ).astype(jnp.bfloat16)
        key_rows = matrix_product(first_normalized, full_k).astype(jnp.bfloat16)
        value_rows = (
            matrix_product(first_normalized, complete_value)
            + ADAPTER_SCALE * matrix_product(reduced_value, value_up_adapter)
        ).astype(jnp.bfloat16)
        key_fold = attend_fold(
            query_rows.reshape(local_len, HEADS, HEAD_DIM), query_pos, layout, half_len
        )
        start_carry = (
            jnp.full((local_len, HEADS), NEG_FILL, jnp.float32),
            jnp.zeros((local_len, HEADS), jnp.float32),
            jnp.zeros((local_len, HEADS, HEAD_DIM), jnp.float32),
        )
        key_store = (key_rows, value_rows)
        run_max, run_sum, run_acc = key_fold(
            start_carry,
            (
                lax.all_gather(key_rows, "seq", axis=0, tiled=True),
                lax.all_gather(value_rows, "seq", axis=0, tiled=True),
            ),
            jnp.int32(0),
        )
        mixed_flat = (run_acc / run_sum[..., None]).reshape(local_len, model_width)
        log_total = run_max + jnp.log(run_sum)
        residual = inputs + matrix_product(mixed_flat.astype(jnp.bfloat16), full_o)
        normed_two, unused_scaled, unused_inv = norm_fwd(residual, feedforward_norm_gain)
        pre_act = matrix_product(normed_two.astype(jnp.bfloat16), full_up)
        gelu_value, unused_slope = gelu_parts(pre_act)
        output = residual + matrix_product(gelu_value.astype(jnp.bfloat16), full_down)
        kept_state = (
            first_normalized,
            reduced_query,
            reduced_value,
            query_rows,
            key_store,
            log_total,
            mixed_flat,
            residual,
            pre_act,
        )
        return (unused, (output.astype(jnp.bfloat16), kept_state))

    unused_carry, (layer_out, kept_all) = lax.scan(forward_one, 0, tokens)
    frozen_back = (
        lax.all_gather(query_weight, "batch", axis=0, tiled=True),
        lax.all_gather(key_weight, "batch", axis=0, tiled=True),
        lax.all_gather(value_weight, "batch", axis=0, tiled=True),
        lax.all_gather(attention_output_weight, "batch", axis=0, tiled=True),
        lax.all_gather(up_weight, "batch", axis=0, tiled=True),
        lax.all_gather(down_weight, "batch", axis=0, tiled=True),
    )

    def backward_one(totals, pieces):
        token_block, cot_block, kept_state = pieces
        (
            first_normalized,
            reduced_query,
            reduced_value,
            query_rows,
            key_store,
            log_total,
            mixed_flat,
            residual,
            pre_act,
        ) = kept_state
        complete_query, full_k, complete_value, full_o, full_up, full_down = frozen_back
        unused_value, gelu_slope = gelu_parts(pre_act)
        pre_grad = (gelu_slope * contracted_against(cot_block, full_down)).astype(jnp.bfloat16)
        resid_grad = cot_block.astype(jnp.float32) + norm_back(
            residual, feedforward_norm_gain, contracted_against(pre_grad, full_up)
        )
        mixed_grad = contracted_against(resid_grad.astype(jnp.bfloat16), full_o).astype(
            jnp.bfloat16
        )
        grad_heads = mixed_grad.reshape(local_len, HEADS, HEAD_DIM)
        row_delta = jnp.sum(
            (mixed_grad.astype(jnp.float32) * mixed_flat).reshape(local_len, HEADS, HEAD_DIM),
            axis=-1,
        )
        query_heads = query_rows.reshape(local_len, HEADS, HEAD_DIM)
        key_fold = grad_fold(
            query_heads, query_pos, grad_heads, log_total, row_delta, layout, half_len
        )
        start_carry = (
            jnp.zeros((local_len, HEADS, HEAD_DIM), jnp.float32),
            jnp.zeros((total_len, model_width), jnp.float32),
            jnp.zeros((total_len, model_width), jnp.float32),
        )
        grad_query, key_part, value_part = key_fold(
            start_carry,
            (
                lax.all_gather(key_store[0], "seq", axis=0, tiled=True),
                lax.all_gather(key_store[1], "seq", axis=0, tiled=True),
            ),
            jnp.int32(0),
        )
        key_sum, value_sum = (
            lax.psum_scatter(
                key_part.astype(jnp.bfloat16), "seq", scatter_dimension=0, tiled=True
            ).astype(jnp.float32),
            lax.psum_scatter(
                value_part.astype(jnp.bfloat16), "seq", scatter_dimension=0, tiled=True
            ).astype(jnp.float32),
        )
        query_reduced = grad_query.reshape(local_len, model_width).astype(jnp.bfloat16)
        key_low = key_sum.astype(jnp.bfloat16)
        value_reduced = value_sum.astype(jnp.bfloat16)
        reduced_query_gradient = (
            ADAPTER_SCALE * contracted_against(query_reduced, query_up_adapter)
        ).astype(jnp.bfloat16)
        reduced_value_gradient = (
            ADAPTER_SCALE * contracted_against(value_reduced, value_up_adapter)
        ).astype(jnp.bfloat16)
        grad_qa = across_documents(first_normalized, reduced_query_gradient)
        query_up_gradient = ADAPTER_SCALE * across_documents(reduced_query, query_reduced)
        grad_va = across_documents(first_normalized, reduced_value_gradient)
        value_up_gradient = ADAPTER_SCALE * across_documents(reduced_value, value_reduced)
        first_norm_gradient = (
            contracted_against(query_reduced, complete_query)
            + contracted_against(key_low, full_k)
            + contracted_against(value_reduced, complete_value)
        )
        first_norm_gradient = (
            first_norm_gradient
            + contracted_against(reduced_query_gradient, query_down_adapter)
            + contracted_against(reduced_value_gradient, value_down_adapter)
        )
        input_grad = resid_grad + norm_back(
            token_block.astype(jnp.float32), attention_norm_gain, first_norm_gradient
        )
        totals = (
            totals[0] + grad_qa,
            totals[1] + query_up_gradient,
            totals[2] + grad_va,
            totals[3] + value_up_gradient,
        )
        return (totals, input_grad.astype(jnp.bfloat16))

    zero_filled = (
        jnp.zeros(query_down_adapter.shape, jnp.float32),
        jnp.zeros(query_up_adapter.shape, jnp.float32),
        jnp.zeros(value_down_adapter.shape, jnp.float32),
        jnp.zeros(value_up_adapter.shape, jnp.float32),
    )
    totals, input_grad = lax.scan(backward_one, zero_filled, (tokens, cotangent, kept_all))
    summed = lax.psum((totals[0], totals[1], totals[2], totals[3]), ("batch", "seq"))
    return (layer_out, input_grad, summed[0], summed[1], summed[2], summed[3])


def solution(mesh):
    return jax.shard_map(
        local,
        mesh=mesh,
        in_specs=(
            P("batch", "seq", None),
            P("batch", "seq", None),
            P(),
            P(),
            P(),
            P("batch", None),
            P("batch", None),
            P("batch", None),
            P("batch", None),
            P("batch", None),
            P("batch", None),
            P(),
            P(),
            P(),
            P(),
        ),
        out_specs=(P("batch", "seq", None), P("batch", "seq", None), P(), P(), P(), P()),
        check_vma=False,
    )
```

profile of v0, /device:TPU:1, one launch (start us, length us, event | category | flops | bytes accessed | tf_op | source)
XLA Modules:
  0.0 1359.9 jit_solution(5179212505656271706)
XLA Ops:
  12.6 41.5 %all-gather.19.cloned.1.call-done = bf16[1024,1024]{1,0:T(8,128)(2,1)} async-done(((bf16[64,1024]{1,0:T(8,128)(2,1)}), bf16[1024,1024]{1,0:T(8,128)(2,1)}) %all-gather.19.cloned.1.call-update) | async-done | bytes 2097168 | tf_op jit(solution)/shard_map/all_gather | solution.py:153
  54.1 42.4 %all-gather.21.cloned.1.call-done = bf16[1024,1024]{1,0:T(8,128)(2,1)} async-done(((bf16[64,1024]{1,0:T(8,128)(2,1)}), bf16[1024,1024]{1,0:T(8,128)(2,1)}) %all-gather.21.cloned.1.call-update) | async-done | bytes 2097168 | tf_op jit(solution)/shard_map/all_gather | solution.py:152
  96.5 42.4 %all-gather.23.cloned.1.call-done = bf16[1024,1024]{1,0:T(8,128)(2,1)} async-done(((bf16[64,1024]{1,0:T(8,128)(2,1)}), bf16[1024,1024]{1,0:T(8,128)(2,1)}) %all-gather.23.cloned.1.call-update) | async-done | bytes 2097168 | tf_op jit(solution)/shard_map/all_gather | solution.py:151
  138.8 42.2 %all-gather.25.cloned.1.call-done = bf16[1024,1024]{1,0:T(8,128)(2,1)} async-done(((bf16[64,1024]{1,0:T(8,128)(2,1)}), bf16[1024,1024]{1,0:T(8,128)(2,1)}) %all-gather.25.cloned.1.call-update) | async-done | bytes 2097168 | tf_op jit(solution)/shard_map/all_gather | solution.py:154
  181.0 75.7 %all-gather.27.cloned.1.call-done = bf16[1024,4096]{1,0:T(8,128)(2,1)} async-done(((bf16[64,4096]{1,0:T(8,128)(2,1)}), bf16[1024,4096]{1,0:T(8,128)(2,1)}) %all-gather.27.cloned.1.call-update) | async-done | bytes 8388624 | tf_op jit(solution)/shard_map/all_gather | solution.py:155
  256.8 75.2 %all-gather.29.cloned.1.call-done = bf16[4096,1024]{1,0:T(8,128)(2,1)} async-done(((bf16[256,1024]{1,0:T(8,128)(2,1)}), bf16[4096,1024]{1,0:T(8,128)(2,1)}) %all-gather.29.cloned.1.call-update) | async-done | bytes 8388624 | tf_op jit(solution)/shard_map/all_gather | solution.py:156
  342.4 346.5 %while.53 = (s32[]{:T(128)}, bf16[3,512,1024]{2,1,0:T(8,128)(2,1)}, bf16[3,512,1024]{2,1,0:T(8,128)(2,1)}, bf16[3,512,4]{1,2,0:T(4,128)(2,1)}, bf16[3,512,4]{1,2...) while((s32[]{:T(128)}, bf16[3,512,1024]{2,1,0:T(8,128)(2,1)}, ...), condition=%wide.region_9.10_spmd, body=%wide.region_1.9_spmd.sunk | while | flops 15180275712 | bytes 289872448 | solution.py:219
  354.0 3.4 fusion.307
  365.8 12.0 all-gather.31.cloned.1.call-done
  377.8 3.9 copy.80
  381.7 15.7 %fusion.308 = (f32[512,16]{0,1:T(8,128)S(1)}, f32[16,1024,512]{2,1,0:T(8,128)}) fusion(pred[512,1024]{0,1:T(8,128)(4,1)} %broadcast_compare_fusion.4, bf16[1024,16,64]{0,2,1:T(8,128)(2,1)} %bitcast.413, bf16[512,16,64]{0,2,1:T(8,128)(2,1)} %bitcast.420), kind=kOutput, calls=%fused_computation.4.clone.1 | convolution fusion | flops 1098899456 | bytes 37257216 | tf_op jit(solution)/shard_map/while/body/eval_jaxpr/qhd,khd->qhk/dot_general | solution.py:70
  397.4 14.3 %fusion.309 = f32[512,16]{0,1:T(8,128)S(1)} fusion(f32[16,1024,512]{2,1,0:T(8,128)} %get-tuple-element.1541, f32[512,16]{0,1:T(8,128)S(1)} %broadcast_maximum_fusion.2, pred[512,1024]{0,1:T(8,128)(4,1)S(1)} %copy-done.6), kind=kLoop, calls=%fused_computation.2.clone.1 | loop fusion | flops 33546240 | bytes 34144256 | tf_op jit(solution)/shard_map/while/body/eval_jaxpr/reduce_sum | solution.py:88
  412.5 3.9 copy.82
  416.4 16.3 %fusion.311 = (bf16[512,16,64]{0,2,1:T(8,128)(2,1)S(1)}, f32[512,16,64]{0,2,1:T(8,128)}) fusion(f32[512,16]{0,1:T(8,128)S(1)} %fusion.309, bf16[1024,16,64]{0,2,1:T(8,128)(2,1)} %bitcast.423, f32[16,1024,512]{2,1,0:T(8,128)} %get-tuple-element.1541, f32[512,16]{0,1:T(8,128)S(1)} %broadcast_maximum_fusion.2, ...), kind=kOutput, calls=%fused_computation.210.clone.1 | convolution fusion | flops 1108344832 | bytes 39387136 | tf_op jit(solution)/shard_map/while/body/eval_jaxpr/qhk,khd->qhd/dot_general | solution.py:89
  439.6 10.9 bitcast_dynamic-update-slice_fusion.21
  450.6 6.1 fusion.313
  468.1 3.5 fusion.307
  480.0 14.1 %all-gather.31.cloned.1.call-done = bf16[1024,1024]{1,0:T(8,128)(2,1)} async-done(((bf16[512,1024]{1,0:T(8,128)(2,1)}), bf16[1024,1024]{1,0:T(8,128)(2,1)}) %all-gather.31.cloned.1.call-update) | async-done | bytes 2097168 | tf_op jit(solution)/shard_map/while/body/eval_jaxpr/all_gather | solution.py:194
  494.1 3.9 copy.80
  498.0 15.6 %fusion.308 = (f32[512,16]{0,1:T(8,128)S(1)}, f32[16,1024,512]{2,1,0:T(8,128)}) fusion(pred[512,1024]{0,1:T(8,128)(4,1)} %broadcast_compare_fusion.4, bf16[1024,16,64]{0,2,1:T(8,128)(2,1)} %bitcast.413, bf16[512,16,64]{0,2,1:T(8,128)(2,1)} %bitcast.420), kind=kOutput, calls=%fused_computation.4.clone.1 | convolution fusion | flops 1098899456 | bytes 37257216 | tf_op jit(solution)/shard_map/while/body/eval_jaxpr/qhd,khd->qhk/dot_general | solution.py:70
  513.7 14.3 %fusion.309 = f32[512,16]{0,1:T(8,128)S(1)} fusion(f32[16,1024,512]{2,1,0:T(8,128)} %get-tuple-element.1541, f32[512,16]{0,1:T(8,128)S(1)} %broadcast_maximum_fusion.2, pred[512,1024]{0,1:T(8,128)(4,1)S(1)} %copy-done.6), kind=kLoop, calls=%fused_computation.2.clone.1 | loop fusion | flops 33546240 | bytes 34144256 | tf_op jit(solution)/shard_map/while/body/eval_jaxpr/reduce_sum | solution.py:88
  528.7 3.9 copy.82
  532.6 16.3 %fusion.311 = (bf16[512,16,64]{0,2,1:T(8,128)(2,1)S(1)}, f32[512,16,64]{0,2,1:T(8,128)}) fusion(f32[512,16]{0,1:T(8,128)S(1)} %fusion.309, bf16[1024,16,64]{0,2,1:T(8,128)(2,1)} %bitcast.423, f32[16,1024,512]{2,1,0:T(8,128)} %get-tuple-element.1541, f32[512,16]{0,1:T(8,128)S(1)} %broadcast_maximum_fusion.2, ...), kind=kOutput, calls=%fused_computation.210.clone.1 | convolution fusion | flops 1108344832 | bytes 39387136 | tf_op jit(solution)/shard_map/while/body/eval_jaxpr/qhk,khd->qhd/dot_general | solution.py:89
  555.8 10.8 bitcast_dynamic-update-slice_fusion.21
  566.6 6.1 fusion.313
  584.3 3.5 fusion.307
  596.2 14.0 %all-gather.31.cloned.1.call-done = bf16[1024,1024]{1,0:T(8,128)(2,1)} async-done(((bf16[512,1024]{1,0:T(8,128)(2,1)}), bf16[1024,1024]{1,0:T(8,128)(2,1)}) %all-gather.31.cloned.1.call-update) | async-done | bytes 2097168 | tf_op jit(solution)/shard_map/while/body/eval_jaxpr/all_gather | solution.py:194
  610.2 3.9 copy.80
  614.1 15.6 %fusion.308 = (f32[512,16]{0,1:T(8,128)S(1)}, f32[16,1024,512]{2,1,0:T(8,128)}) fusion(pred[512,1024]{0,1:T(8,128)(4,1)} %broadcast_compare_fusion.4, bf16[1024,16,64]{0,2,1:T(8,128)(2,1)} %bitcast.413, bf16[512,16,64]{0,2,1:T(8,128)(2,1)} %bitcast.420), kind=kOutput, calls=%fused_computation.4.clone.1 | convolution fusion | flops 1098899456 | bytes 37257216 | tf_op jit(solution)/shard_map/while/body/eval_jaxpr/qhd,khd->qhk/dot_general | solution.py:70
  629.8 14.3 %fusion.309 = f32[512,16]{0,1:T(8,128)S(1)} fusion(f32[16,1024,512]{2,1,0:T(8,128)} %get-tuple-element.1541, f32[512,16]{0,1:T(8,128)S(1)} %broadcast_maximum_fusion.2, pred[512,1024]{0,1:T(8,128)(4,1)S(1)} %copy-done.6), kind=kLoop, calls=%fused_computation.2.clone.1 | loop fusion | flops 33546240 | bytes 34144256 | tf_op jit(solution)/shard_map/while/body/eval_jaxpr/reduce_sum | solution.py:88
  644.8 3.9 copy.82
  648.7 16.3 %fusion.311 = (bf16[512,16,64]{0,2,1:T(8,128)(2,1)S(1)}, f32[512,16,64]{0,2,1:T(8,128)}) fusion(f32[512,16]{0,1:T(8,128)S(1)} %fusion.309, bf16[1024,16,64]{0,2,1:T(8,128)(2,1)} %bitcast.423, f32[16,1024,512]{2,1,0:T(8,128)} %get-tuple-element.1541, f32[512,16]{0,1:T(8,128)S(1)} %broadcast_maximum_fusion.2, ...), kind=kOutput, calls=%fused_computation.210.clone.1 | convolution fusion | flops 1108344832 | bytes 39387136 | tf_op jit(solution)/shard_map/while/body/eval_jaxpr/qhk,khd->qhd/dot_general | solution.py:89
  672.0 10.8 bitcast_dynamic-update-slice_fusion.21
  682.8 6.1 fusion.313
  691.0 528.1 %while.54 = (s32[]{:T(128)}, f32[1024,4]{0,1:T(4,128)S(1)}, f32[4,1024]{1,0:T(4,128)S(1)}, f32[1024,4]{0,1:T(4,128)S(1)}, f32[4,1024]{1,0:T(4,128)S(1)}, /*index...) while((s32[]{:T(128)}, f32[1024,4]{0,1:T(4,128)S(1)}, ...), condition=%wide.region_23.24_spmd.clone, body=%wide.region_10.23_spmd.clone.sunk | while | flops 18439802880 | bytes 411029760 | solution.py:321
  732.3 19.2 %multiply_reduce_fusion.9 = (f32[512]{0:T(512)S(1)}, f32[512]{0:T(512)S(1)}, f32[512,1024]{1,0:T(8,128)}) fusion(f32[1024]{0:T(1024)S(1)} %get-tuple-element.1768, f32[512]{0:T(512)S(1)} %add_rsqrt_fusion.10, f32[512]{0:T(512)S(1)} %broadcast_multiply_fusion.17, f32[3,512,1024]{2,1,0:T(8,128)} %get-tuple-element.1764, s32[]{:T(128)S(6)} %copy.143, ...), kind=kOutput, calls=%fused_computation.130.clone.1 | convolution fusion | flops 8630829056 | bytes 30422528 | tf_op jit(solution)/shard_map/while/body/eval_jaxpr/dot_general | solution.py:22
  751.5 3.4 multiply_add_fusion.4
  767.8 17.5 %fusion.351 = f32[16,1024,512]{2,1,0:T(8,128)} fusion(bf16[1024,16,64]{0,2,1:T(8,128)(2,1)} %bitcast.411, bf16[512,16,64]{0,2,1:T(8,128)(2,1)} %bitcast.414), kind=kOutput, calls=%fused_computation.214.clone.1 | convolution fusion | flops 1073741824 | bytes 36700160 | tf_op jit(solution)/shard_map/while/body/eval_jaxpr/qhd,khd->qhk/dot_general | solution.py:70
  785.3 16.0 %fusion.356 = bf16[16,64,1024]{2,1,0:T(8,128)(2,1)} fusion(bf16[512,16,64]{0,2,1:T(8,128)(2,1)} %bitcast.424, f32[16,1024,512]{2,1,0:T(8,128)} %fusion.351, f32[512,16]{0,1:T(8,128)S(1)} %dynamic-slice_bitcast_fusion.2, pred[512,1024]{0,1:T(8,128)(4,1)} %broadcast_compare_fusion.5), kind=kOutput, calls=%fused_computation.129.clone.1 | convolution fusion | flops 1108344832 | bytes 37257216 | tf_op jit(solution)/shard_map/while/body/eval_jaxpr/qhk,qhd->khd/dot_general | solution.py:117
  806.2 21.4 %fusion.353 = bf16[512,16,1024]{0,2,1:T(8,128)(2,1)} fusion(f32[16,1024,512]{2,1,0:T(8,128)} %fusion.351, f32[512,16]{0,1:T(8,128)S(1)} %bitcast_reduce_fusion.2, f32[512,16]{0,1:T(8,128)S(1)} %dynamic-slice_bitcast_fusion.2, pred[512,1024]{0,1:T(8,128)(4,1)} %broadcast_compare_fusion.5, bf16[1024,16,64]{0,2,1:T(8,128)(2,1)} %bitcast.429, ...), kind=kOutput, calls=%fused_computation.80.clone.1 | convolution fusion | flops 1124073472 | bytes 54067200 | tf_op jit(solution)/shard_map/while/body/eval_jaxpr/qhd,khd->qhk/dot_general | solution.py:110
  827.5 12.6 multiply_convert_fusion.7
  841.8 9.2 multiply_convert_fusion.6
  859.9 4.6 fusion.361
  864.6 7.7 reduce-scatter.5.cloned.1.call-done
  872.3 3.4 fusion.363
  901.1 19.2 %multiply_reduce_fusion.9 = (f32[512]{0:T(512)S(1)}, f32[512]{0:T(512)S(1)}, f32[512,1024]{1,0:T(8,128)}) fusion(f32[1024]{0:T(1024)S(1)} %get-tuple-element.1768, f32[512]{0:T(512)S(1)} %add_rsqrt_fusion.10, f32[512]{0:T(512)S(1)} %broadcast_multiply_fusion.17, f32[3,512,1024]{2,1,0:T(8,128)} %get-tuple-element.1764, s32[]{:T(128)S(6)} %copy.143, ...), kind=kOutput, calls=%fused_computation.130.clone.1 | convolution fusion | flops 8630829056 | bytes 30422528 | tf_op jit(solution)/shard_map/while/body/eval_jaxpr/dot_general | solution.py:22
  920.3 3.4 multiply_add_fusion.4
  936.6 17.5 %fusion.351 = f32[16,1024,512]{2,1,0:T(8,128)} fusion(bf16[1024,16,64]{0,2,1:T(8,128)(2,1)} %bitcast.411, bf16[512,16,64]{0,2,1:T(8,128)(2,1)} %bitcast.414), kind=kOutput, calls=%fused_computation.214.clone.1 | convolution fusion | flops 1073741824 | bytes 36700160 | tf_op jit(solution)/shard_map/while/body/eval_jaxpr/qhd,khd->qhk/dot_general | solution.py:70
  954.1 16.0 %fusion.356 = bf16[16,64,1024]{2,1,0:T(8,128)(2,1)} fusion(bf16[512,16,64]{0,2,1:T(8,128)(2,1)} %bitcast.424, f32[16,1024,512]{2,1,0:T(8,128)} %fusion.351, f32[512,16]{0,1:T(8,128)S(1)} %dynamic-slice_bitcast_fusion.2, pred[512,1024]{0,1:T(8,128)(4,1)} %broadcast_compare_fusion.5), kind=kOutput, calls=%fused_computation.129.clone.1 | convolution fusion | flops 1108344832 | bytes 37257216 | tf_op jit(solution)/shard_map/while/body/eval_jaxpr/qhk,qhd->khd/dot_general | solution.py:117
  975.0 21.4 %fusion.353 = bf16[512,16,1024]{0,2,1:T(8,128)(2,1)} fusion(f32[16,1024,512]{2,1,0:T(8,128)} %fusion.351, f32[512,16]{0,1:T(8,128)S(1)} %bitcast_reduce_fusion.2, f32[512,16]{0,1:T(8,128)S(1)} %dynamic-slice_bitcast_fusion.2, pred[512,1024]{0,1:T(8,128)(4,1)} %broadcast_compare_fusion.5, bf16[1024,16,64]{0,2,1:T(8,128)(2,1)} %bitcast.429, ...), kind=kOutput, calls=%fused_computation.80.clone.1 | convolution fusion | flops 1124073472 | bytes 54067200 | tf_op jit(solution)/shard_map/while/body/eval_jaxpr/qhd,khd->qhk/dot_general | solution.py:110
  996.3 12.6 multiply_convert_fusion.7
  1010.6 9.3 multiply_convert_fusion.6
  1028.7 4.6 fusion.361
  1033.4 7.7 reduce-scatter.5.cloned.1.call-done
  1069.9 19.1 %multiply_reduce_fusion.9 = (f32[512]{0:T(512)S(1)}, f32[512]{0:T(512)S(1)}, f32[512,1024]{1,0:T(8,128)}) fusion(f32[1024]{0:T(1024)S(1)} %get-tuple-element.1768, f32[512]{0:T(512)S(1)} %add_rsqrt_fusion.10, f32[512]{0:T(512)S(1)} %broadcast_multiply_fusion.17, f32[3,512,1024]{2,1,0:T(8,128)} %get-tuple-element.1764, s32[]{:T(128)S(6)} %copy.143, ...), kind=kOutput, calls=%fused_computation.130.clone.1 | convolution fusion | flops 8630829056 | bytes 30422528 | tf_op jit(solution)/shard_map/while/body/eval_jaxpr/dot_general | solution.py:22
  1089.0 3.4 multiply_add_fusion.4
  1105.4 17.5 %fusion.351 = f32[16,1024,512]{2,1,0:T(8,128)} fusion(bf16[1024,16,64]{0,2,1:T(8,128)(2,1)} %bitcast.411, bf16[512,16,64]{0,2,1:T(8,128)(2,1)} %bitcast.414), kind=kOutput, calls=%fused_computation.214.clone.1 | convolution fusion | flops 1073741824 | bytes 36700160 | tf_op jit(solution)/shard_map/while/body/eval_jaxpr/qhd,khd->qhk/dot_general | solution.py:70
  1122.8 16.0 %fusion.356 = bf16[16,64,1024]{2,1,0:T(8,128)(2,1)} fusion(bf16[512,16,64]{0,2,1:T(8,128)(2,1)} %bitcast.424, f32[16,1024,512]{2,1,0:T(8,128)} %fusion.351, f32[512,16]{0,1:T(8,128)S(1)} %dynamic-slice_bitcast_fusion.2, pred[512,1024]{0,1:T(8,128)(4,1)} %broadcast_compare_fusion.5), kind=kOutput, calls=%fused_computation.129.clone.1 | convolution fusion | flops 1108344832 | bytes 37257216 | tf_op jit(solution)/shard_map/while/body/eval_jaxpr/qhk,qhd->khd/dot_general | solution.py:117
  1143.7 21.4 %fusion.353 = bf16[512,16,1024]{0,2,1:T(8,128)(2,1)} fusion(f32[16,1024,512]{2,1,0:T(8,128)} %fusion.351, f32[512,16]{0,1:T(8,128)S(1)} %bitcast_reduce_fusion.2, f32[512,16]{0,1:T(8,128)S(1)} %dynamic-slice_bitcast_fusion.2, pred[512,1024]{0,1:T(8,128)(4,1)} %broadcast_compare_fusion.5, bf16[1024,16,64]{0,2,1:T(8,128)(2,1)} %bitcast.429, ...), kind=kOutput, calls=%fused_computation.80.clone.1 | convolution fusion | flops 1124073472 | bytes 54067200 | tf_op jit(solution)/shard_map/while/body/eval_jaxpr/qhd,khd->qhk/dot_general | solution.py:110
  1165.1 12.6 multiply_convert_fusion.7
  1179.3 9.3 multiply_convert_fusion.6
  1197.5 4.6 fusion.361
  1202.1 7.7 reduce-scatter.5.cloned.1.call-done
  1219.9 127.8 %all-reduce.3.cloned.1.call-done = (f32[1024,4]{0,1:T(4,128)}, f32[4,1024]{1,0:T(4,128)}, f32[1024,4]{0,1:T(4,128)}, f32[4,1024]{1,0:T(4,128)}) async-done(((f32[1024,4]{0,1:T(4,128)}, f32[4,1024]{1,0:T(4,128)}, f32[1024,4]{0,1:T(4,128)}, f32[4,1024]{1,0:T(4,128)}), (f32[1024,4]{0,1:T(4,128)}, f32[4,1024]{1,0:T(4,128)}, f32[1024,4]{0,1:T(4,128)}, f32[4,1024]{1,0:T(4,128)})) %all-reduce.3.cloned.1.call-update) | async-done | bytes 65552 | tf_op jit(solution)/shard_map/psum | solution.py:322
  (415 shorter events, 273.7 us)
Async XLA Ops:
  7.2 46.9 %all-gather.19.cloned.1.call-start = ((), (), s32[]{:S(2)}) async-start(), calls=%async_computation.2 | async-start | bytes 2228224 | tf_op jit(solution)/shard_map/all_gather | solution.py:153
  7.9 88.6 %all-gather.21.cloned.1.call-start = ((), (), s32[]{:S(2)}) async-start(), calls=%async_computation.3 | async-start | bytes 2228224 | tf_op jit(solution)/shard_map/all_gather | solution.py:152
  8.7 130.2 %all-gather.23.cloned.1.call-start = ((), (), s32[]{:S(2)}) async-start(), calls=%async_computation.4 | async-start | bytes 2228224 | tf_op jit(solution)/shard_map/all_gather | solution.py:151
  9.4 171.7 %all-gather.25.cloned.1.call-start = ((), (), s32[]{:S(2)}) async-start(), calls=%async_computation.5 | async-start | bytes 2228224 | tf_op jit(solution)/shard_map/all_gather | solution.py:154
  10.0 246.8 %all-gather.27.cloned.1.call-start = ((), (), s32[]{:S(2)}) async-start(), calls=%async_computation.6 | async-start | bytes 8912896 | tf_op jit(solution)/shard_map/all_gather | solution.py:155
  10.6 321.4 %all-gather.29.cloned.1.call-start = ((), (), s32[]{:S(2)}) async-start(), calls=%async_computation.7 | async-start | bytes 8912896 | tf_op jit(solution)/shard_map/all_gather | solution.py:156
  338.1 4.2 copy-start
  338.1 4.2 copy-start.14
  338.1 4.2 copy-start.15
  338.1 4.2 copy-start.16
  338.1 4.2 copy-start.17
  338.1 4.2 copy-start.18
  338.1 4.2 copy-start.27
  338.2 4.2 copy-start.28
  342.4 35.4 %all-gather.31.cloned.1.call-start = ((), (), s32[]{:S(2)}) async-start(), calls=%async_computation.9 | async-start | bytes 3145728 | tf_op jit(solution)/shard_map/while/body/eval_jaxpr/all_gather | solution.py:194
  346.7 65.8 %all-gather.33.cloned.1.call-start = ((), (), s32[]{:S(2)}) async-start(), calls=%async_computation.10 | async-start | bytes 3145728 | tf_op jit(solution)/shard_map/while/body/eval_jaxpr/all_gather | solution.py:195
  354.0 3.4 copy-start.5
  381.7 15.7 %copy-start.6 = (pred[512,1024]{0,1:T(8,128)(4,1)S(1)}, pred[512,1024]{0,1:T(8,128)(4,1)}, u32[]{:S(2)}) copy-start(pred[512,1024]{0,1:T(8,128)(4,1)} %broadcast_compare_fusion.4) | copy-start | bytes 1572868 | tf_op jit(solution)/shard_map/while
  438.2 12.4 slice-start
  439.6 10.9 slice-start.1
  456.6 37.5 %all-gather.31.cloned.1.call-start = ((), (), s32[]{:S(2)}) async-start(), calls=%async_computation.9 | async-start | bytes 3145728 | tf_op jit(solution)/shard_map/while/body/eval_jaxpr/all_gather | solution.py:194
  460.8 67.8 %all-gather.33.cloned.1.call-start = ((), (), s32[]{:S(2)}) async-start(), calls=%async_computation.10 | async-start | bytes 3145728 | tf_op jit(solution)/shard_map/while/body/eval_jaxpr/all_gather | solution.py:195
  468.1 3.5 copy-start.5
  498.0 15.6 %copy-start.6 = (pred[512,1024]{0,1:T(8,128)(4,1)S(1)}, pred[512,1024]{0,1:T(8,128)(4,1)}, u32[]{:S(2)}) copy-start(pred[512,1024]{0,1:T(8,128)(4,1)} %broadcast_compare_fusion.4) | copy-start | bytes 1572868 | tf_op jit(solution)/shard_map/while
  554.3 12.3 slice-start
  555.8 10.8 slice-start.1
  572.7 37.5 %all-gather.31.cloned.1.call-start = ((), (), s32[]{:S(2)}) async-start(), calls=%async_computation.9 | async-start | bytes 3145728 | tf_op jit(solution)/shard_map/while/body/eval_jaxpr/all_gather | solution.py:194
  576.9 67.8 %all-gather.33.cloned.1.call-start = ((), (), s32[]{:S(2)}) async-start(), calls=%async_computation.10 | async-start | bytes 3145728 | tf_op jit(solution)/shard_map/while/body/eval_jaxpr/all_gather | solution.py:195
  584.2 3.5 copy-start.5
  614.1 15.6 %copy-start.6 = (pred[512,1024]{0,1:T(8,128)(4,1)S(1)}, pred[512,1024]{0,1:T(8,128)(4,1)}, u32[]{:S(2)}) copy-start(pred[512,1024]{0,1:T(8,128)(4,1)} %broadcast_compare_fusion.4) | copy-start | bytes 1572868 | tf_op jit(solution)/shard_map/while
  670.4 12.4 slice-start
  672.0 10.8 slice-start.1
  712.9 55.0 %all-gather.35.cloned.1.call-start = ((), (), s32[]{:S(2)}) async-start(), calls=%async_computation.11 | async-start | bytes 3145728 | tf_op jit(solution)/shard_map/while/body/eval_jaxpr/all_gather | solution.py:268
  717.5 88.7 %all-gather.37.cloned.1.call-start = ((), (), s32[]{:S(2)}) async-start(), calls=%async_computation.12 | async-start | bytes 3145728 | tf_op jit(solution)/shard_map/while/body/eval_jaxpr/all_gather | solution.py:269
  722.1 136.3 %reduce-scatter.3.cloned.1.call-start = ((), (), s32[]{:S(2)}) async-start(), calls=%async_computation.13 | async-start | bytes 3145728 | tf_op jit(solution)/shard_map/while/body/eval_jaxpr/reduce_scatter | solution.py:277
  751.5 3.4 copy-start.8
  751.5 3.8 copy-start.9
  754.9 3.4 copy-start.2
  801.3 71.0 %reduce-scatter.5.cloned.1.call-start = ((), (), s32[]{:S(2)}) async-start(), calls=%async_computation.14 | async-start | bytes 3145728 | tf_op jit(solution)/shard_map/while/body/eval_jaxpr/reduce_scatter | solution.py:274
  851.0 4.7 copy-start.31
  872.3 3.4 copy-start.7
  872.3 3.4 copy-start.11
  872.3 3.8 copy-start.12
  881.7 55.0 %all-gather.35.cloned.1.call-start = ((), (), s32[]{:S(2)}) async-start(), calls=%async_computation.11 | async-start | bytes 3145728 | tf_op jit(solution)/shard_map/while/body/eval_jaxpr/all_gather | solution.py:268
  886.3 88.7 %all-gather.37.cloned.1.call-start = ((), (), s32[]{:S(2)}) async-start(), calls=%async_computation.12 | async-start | bytes 3145728 | tf_op jit(solution)/shard_map/while/body/eval_jaxpr/all_gather | solution.py:269
  890.9 136.4 %reduce-scatter.3.cloned.1.call-start = ((), (), s32[]{:S(2)}) async-start(), calls=%async_computation.13 | async-start | bytes 3145728 | tf_op jit(solution)/shard_map/while/body/eval_jaxpr/reduce_scatter | solution.py:277
  920.3 3.4 copy-start.8
  920.3 3.8 copy-start.9
  923.6 3.4 copy-start.2
  970.1 70.9 %reduce-scatter.5.cloned.1.call-start = ((), (), s32[]{:S(2)}) async-start(), calls=%async_computation.14 | async-start | bytes 3145728 | tf_op jit(solution)/shard_map/while/body/eval_jaxpr/reduce_scatter | solution.py:274
  1019.9 4.8 copy-start.31
  1041.1 3.4 copy-start.11
  1041.1 3.8 copy-start.12
  1050.4 54.9 %all-gather.35.cloned.1.call-start = ((), (), s32[]{:S(2)}) async-start(), calls=%async_computation.11 | async-start | bytes 3145728 | tf_op jit(solution)/shard_map/while/body/eval_jaxpr/all_gather | solution.py:268
  1055.0 88.7 %all-gather.37.cloned.1.call-start = ((), (), s32[]{:S(2)}) async-start(), calls=%async_computation.12 | async-start | bytes 3145728 | tf_op jit(solution)/shard_map/while/body/eval_jaxpr/all_gather | solution.py:269
  1059.7 136.3 %reduce-scatter.3.cloned.1.call-start = ((), (), s32[]{:S(2)}) async-start(), calls=%async_computation.13 | async-start | bytes 3145728 | tf_op jit(solution)/shard_map/while/body/eval_jaxpr/reduce_scatter | solution.py:277
  1089.0 3.4 copy-start.8
  1089.0 3.8 copy-start.9
  1092.4 3.4 copy-start.2
  1138.9 70.9 %reduce-scatter.5.cloned.1.call-start = ((), (), s32[]{:S(2)}) async-start(), calls=%async_computation.14 | async-start | bytes 3145728 | tf_op jit(solution)/shard_map/while/body/eval_jaxpr/reduce_scatter | solution.py:274
  1188.6 4.8 copy-start.31
  1209.8 3.4 copy-start.11
  1209.8 3.8 copy-start.12
  1219.2 128.5 %all-reduce.3.cloned.1.call-start = ((), (), s32[]{:S(2)}) async-start(), calls=%async_computation.8 | async-start | bytes 131072 | tf_op jit(solution)/shard_map/psum | solution.py:322
  (29 other events, 59.5 us)
Sparse Core Ops, SparseCore 0:
  10.2 43.8 all-gather.18
  56.3 40.1 all-gather.20
  98.6 40.1 all-gather.22
  140.8 40.1 all-gather.24
  183.1 73.6 all-gather.26
  258.8 73.1 all-gather.28
  346.8 30.9 all-gather.30
  379.3 33.1 all-gather.32
  461.0 33.1 all-gather.30
  495.5 33.1 all-gather.32
  577.0 33.1 all-gather.30
  611.6 33.1 all-gather.32
  717.6 33.1 all-gather.34
  752.2 33.1 all-gather.36
  801.4 31.9 reduce-scatter.2
  840.3 31.9 reduce-scatter.4
  886.4 33.1 all-gather.34
  920.9 33.1 all-gather.36
  970.2 31.8 reduce-scatter.2
  1009.1 31.9 reduce-scatter.4
  1055.2 33.0 all-gather.34
  1089.8 33.1 all-gather.36
  1139.0 31.8 reduce-scatter.2
  1177.8 31.8 reduce-scatter.4
  1226.8 120.8 all-reduce.2
where the time goes:
time: 1380 us; the launch traced here: 1360 us
  matrix products  562 us (41%)
  waiting for transfers between devices  516 us (37%)
  local copies, waits for them, and re-layouts  142 us (10%)
  other arithmetic  100 us (7%)
  loops' own time  22.9 us (2%)
  between operations  14.4 us (1%)
    psum x1, waiting for transfers between devices, local(): lax.psum((totals[0], totals[1], totals[2], totals[3]), ('batch', 'seq'))  128 us
    dot_general x27, matrix products, contracted_against(): lax.dot_general(left_op, right_op, (((1,), (1,)), ((), ())), preferred_el...  113 us
    dot_general x30, matrix products, matrix_product(): return jnp.dot(left_op, right_op, preferred_element_type=jnp.float32)  108 us
    dot_general x6, matrix products, masked_scores(): jnp.einsum('qhd,khd->qhk', query_heads, key_heads, preferred_element_type...  99.3 us
    all_gather x1, waiting for transfers between devices, local(): lax.all_gather(up_weight, 'batch', axis=0, tiled=True)  75.7 us
    all_gather x1, waiting for transfers between devices, local(): lax.all_gather(down_weight, 'batch', axis=0, tiled=True)  75.2 us
    dot_general x3, matrix products, key_fold(): jnp.einsum('qhd,khd->qhk', grad_heads, value_heads, preferred_element_typ...  64.1 us
    dot_general x3, matrix products, key_fold(): jnp.einsum('qhk,khd->qhd', weights_now.astype(jnp.bfloat16), value_heads,...  48.9 us
  transfers between devices with their start and end apart: 25, of which 16 were waited for; matrix products, arithmetic and copies ran while one was open for 44% of the time, Pallas kernels for 0%

commit v1 on v0

v1 whole, which is shorter than its diff:
```python
import functools
import math

import jax
import jax.numpy as jnp
from jax import lax
from jax.experimental import pallas as pl
from jax.experimental.pallas import tpu as pltpu
from jax.sharding import PartitionSpec as P


LOG2E = math.log2(math.e)
SCALE = 0.125
NT = (((1,), (1,)), ((), ()))
NN = (((1,), (0,)), ((), ()))
F32 = jnp.float32
BF = jnp.bfloat16

def dot(a, b, dims=NN):
    return lax.dot_general(a, b, dims, preferred_element_type=F32)

def in_order(ref, where, blocks, size):
    halves, rows = ref.shape[0], ref.shape[2]
    per = rows // size
    out = []
    for p in range(blocks):
        s = where[p]
        out.append(ref[s // per, 0, pl.ds(pl.multiple_of((s % per) * size, size), size), :])
    return jnp.concatenate(out, axis=0)

def att_fwd_kernel(where, q_ref, k_ref, v_ref, o_ref, lse_ref, *, blocks, size, tile):
    q = in_order(q_ref, where, blocks, size)
    k = in_order(k_ref, where, blocks, size)
    v = in_order(v_ref, where, blocks, size)
    n = blocks * size
    vt = v.T
    lane = lax.broadcasted_iota(jnp.int32, (1, 128), 1)
    c = SCALE * LOG2E
    tri = lax.broadcasted_iota(jnp.int32, (tile, tile), 0) <= lax.broadcasted_iota(jnp.int32, (tile, tile), 1)
    work = [(i, h) for i in range(n // tile) for h in range(2)]
    lses = [[], []]
    ots = {}

    def scores(i, h):
        qm = jnp.where((lane < 64) == (h == 0), q[i * tile:(i + 1) * tile], jnp.zeros((), BF))
        return dot(k[:(i + 1) * tile], qm, NT)

    ahead = scores(*work[0])
    for t, (i, h) in enumerate(work):
        st = ahead
        if t + 1 < len(work):
            ahead = scores(*work[t + 1])
        kk = (i + 1) * tile
        diag = jnp.where(tri, st[i * tile:], -1e30)
        st = diag if i == 0 else jnp.concatenate([st[: i * tile], diag], axis=0)
        m = jnp.max(st, axis=0, keepdims=True) * c
        e = jnp.exp2(st * c - m)
        l = jnp.sum(e, axis=0, keepdims=True)
        o = dot(vt[64 * h:64 * h + 64, :kk], e.astype(BF))
        ots[i, h] = o * (1.0 / l)
        lses[h].append(m + jnp.log2(l))
    outs = [jnp.concatenate([ots[i, 0], ots[i, 1]], axis=0).T.astype(BF) for i in range(n // tile)]
    o = jnp.concatenate(outs, axis=0)
    halves, rows = o_ref.shape[0], o_ref.shape[2]
    per = rows // size
    for p in range(blocks):
        s = where[p]
        o_ref[s // per, 0, pl.ds(pl.multiple_of((s % per) * size, size), size), :] = o[p * size:(p + 1) * size]
    for h in range(2):
        lse_ref[0, 0, h:h + 1, :] = jnp.concatenate(lses[h], axis=1)

def att_fwd(where, qkv, size, tile=256):
    halves, docs, rows, w3 = qkv.shape
    w = w3 // 3
    pairs = w // 128
    n = halves * rows
    blocks = n // size
    def spec(part):
        return pl.BlockSpec((halves, 1, rows, 128), lambda d, p, s, part=part: (0, d, 0, part * pairs + p))
    return pl.pallas_call(
        functools.partial(att_fwd_kernel, blocks=blocks, size=size, tile=tile),
        grid_spec=pltpu.PrefetchScalarGridSpec(
            num_scalar_prefetch=1, grid=(docs, pairs),
            in_specs=[spec(0), spec(1), spec(2)],
            out_specs=[pl.BlockSpec((halves, 1, rows, 128), lambda d, p, s: (0, d, 0, p)),
                       pl.BlockSpec((1, 1, 2, n), lambda d, p, s: (d, p, 0, 0))]),
        out_shape=[jax.ShapeDtypeStruct((halves, docs, rows, w), BF),
                   jax.ShapeDtypeStruct((docs, pairs, 2, n), F32)],
        compiler_params=pltpu.CompilerParams(vmem_limit_bytes=60 << 20),
        name="attention_forward",
    )(where, qkv, qkv, qkv)

def att_bwd_kernel(where, q_ref, k_ref, v_ref, o_ref, g_ref, lse_ref, dq_ref, dk_ref, dv_ref, dqt, *, blocks, size, tile):
    q = in_order(q_ref, where, blocks, size)
    k = in_order(k_ref, where, blocks, size)
    v = in_order(v_ref, where, blocks, size)
    o = in_order(o_ref, where, blocks, size)
    g = in_order(g_ref, where, blocks, size)
    n = blocks * size
    kt = k.T
    lane = lax.broadcasted_iota(jnp.int32, (1, 128), 1)
    c = SCALE * LOG2E
    tri = lax.broadcasted_iota(jnp.int32, (tile, tile), 0) <= lax.broadcasted_iota(jnp.int32, (tile, tile), 1)
    prod = (o.astype(F32) * g.astype(F32)).astype(BF)
    sel = (lax.broadcasted_iota(jnp.int32, (8, 128), 1) // 64 == lax.broadcasted_iota(jnp.int32, (8, 128), 0)).astype(BF)
    delta = dot(sel, prod, NT)
    zero = jnp.zeros((), BF)
    masks = [(lane < 64) == (h == 0) for h in range(2)]
    qms = [jnp.where(mk, q, zero) for mk in masks]
    gms = [jnp.where(mk, g, zero) for mk in masks]
    lse = lse_ref[0, 0]
    halves, rows = o_ref.shape[0], o_ref.shape[2]
    per = rows // size
    dks, dvs = [], []
    work = [(j, h) for j in range(n // tile) for h in range(2)]

    def products(j, h):
        lo, hi = j * tile, (j + 1) * tile
        return dot(k[lo:hi], qms[h][lo:], NT), dot(v[lo:hi], gms[h][lo:], NT)

    ahead = products(*work[0])
    for t, (j, h) in enumerate(work):
        st, dp = ahead
        if t + 1 < len(work):
            ahead = products(*work[t + 1])
        lo, hi = j * tile, (j + 1) * tile
        p = jnp.exp2(st * c - lse[h:h + 1, lo:])
        dg = jnp.where(tri, p[:, :tile], 0.0)
        p = dg if hi == n else jnp.concatenate([dg, p[:, tile:]], axis=1)
        ds = (p * (dp - delta[h:h + 1, lo:])).astype(BF)
        dvh = dot(p.astype(BF), gms[h][lo:])
        dkh = dot(ds, qms[h][lo:])
        dv = dvh if h == 0 else dv + dvh
        dk = dkh if h == 0 else dk + dkh
        dqh = dot(kt[64 * h:64 * h + 64, lo:hi], ds)
        if j == 0:
            dqt[64 * h:64 * h + 64, :] = dqh
        else:
            dqt[64 * h:64 * h + 64, lo:] += dqh
        if h == 1:
            dks.append((dk * SCALE).astype(BF))
            dvs.append(dv.astype(BF))
    dk = jnp.concatenate(dks, axis=0)
    dv = jnp.concatenate(dvs, axis=0)
    dq = (dqt[...] * SCALE).T.astype(BF)
    for p in range(blocks):
        s = where[p]
        at = (s // per, 0, pl.ds(pl.multiple_of((s % per) * size, size), size), slice(None))
        piece = slice(p * size, (p + 1) * size)
        dq_ref[at] = dq[piece]
        dk_ref[at] = dk[piece]
        dv_ref[at] = dv[piece]

def att_bwd(where, qkv, o, g, lse, size, tile=256):
    halves, docs, rows, w3 = qkv.shape
    w = w3 // 3
    pairs = w // 128
    n = halves * rows
    blocks = n // size
    def spec(part):
        return pl.BlockSpec((halves, 1, rows, 128), lambda d, p, s, part=part: (0, d, 0, part * pairs + p))
    return pl.pallas_call(
        functools.partial(att_bwd_kernel, blocks=blocks, size=size, tile=tile),
        grid_spec=pltpu.PrefetchScalarGridSpec(
            num_scalar_prefetch=1, grid=(docs, pairs),
            in_specs=[spec(0), spec(1), spec(2), spec(0), spec(0),
                      pl.BlockSpec((1, 1, 2, n), lambda d, p, s: (d, p, 0, 0))],
            out_specs=[spec(0)] * 3,
            scratch_shapes=[pltpu.VMEM((128, n), F32)]),
        out_shape=[jax.ShapeDtypeStruct((halves, docs, rows, w), BF)] * 3,
        compiler_params=pltpu.CompilerParams(vmem_limit_bytes=60 << 20),
        name="attention_backward",
    )(where, qkv, qkv, qkv, o, g, lse)
EPS = 1e-5
GELU_C = 0.7978845608028654
TN = (((0,), (0,)), ((), ()))

def normalise(x):
    mean = jnp.mean(x, axis=-1, keepdims=True)
    cen = x - mean
    inv = lax.rsqrt(jnp.mean(cen * cen, axis=-1, keepdims=True) + EPS)
    return cen * inv, inv

def norm_back(xh, inv, gain, up):
    t = up * gain
    return inv * (t - jnp.mean(t, axis=-1, keepdims=True) - xh * jnp.mean(t * xh, axis=-1, keepdims=True))

def gelu_parts(u):
    cubic = 0.044715 * u * u
    th = jnp.tanh(GELU_C * (u + cubic * u))
    half = 0.5 * (1.0 + th)
    return half * u, half + (0.5 * GELU_C) * u * (1.0 - th * th) * (1.0 + 3.0 * cubic)

def project_kernel(x_ref, gain_ref, w_ref, down_ref, up_ref, out_ref, low_ref):
    groups, w3 = out_ref.shape[0], out_ref.shape[3]
    w = w3 // 3
    xh, _ = normalise(x_ref[0].astype(F32))
    n1 = (xh * gain_ref[...]).astype(BF)
    low = dot(n1, down_ref[...]).astype(BF)
    low_ref[0] = low
    for g in range(groups):
        for part in range(3):
            cols = slice(g * w3 + part * w, g * w3 + (part + 1) * w)
            y = dot(n1, w_ref[:, cols])
            if part != 1:
                y = y + dot(low, up_ref[:, cols])
            out_ref[g, 0, :, part * w:(part + 1) * w] = y.astype(BF)

def project(x, gain, w, down, up, groups):
    docs, rows, d = x.shape
    n = w.shape[1]
    full = lambda a: pl.BlockSpec(a.shape, lambda i: (0,) * a.ndim)
    return pl.pallas_call(
        project_kernel,
        grid=(docs,),
        in_specs=[pl.BlockSpec((1, rows, d), lambda i: (i, 0, 0)), full(gain), full(w), full(down), full(up)],
        out_specs=[pl.BlockSpec((groups, 1, rows, n // groups), lambda i: (0, i, 0, 0)),
                   pl.BlockSpec((1, rows, 128), lambda i: (i, 0, 0))],
        out_shape=[jax.ShapeDtypeStruct((groups, docs, rows, n // groups), BF),
                   jax.ShapeDtypeStruct((docs, rows, 128), BF)],
        compiler_params=pltpu.CompilerParams(vmem_limit_bytes=60 << 20),
        name="projections",
    )(x, gain, w, down, up)

def middle_kernel(x_ref, att_ref, cot_ref, gain_ref, wo_ref, up_ref, down_ref, out_ref, res_ref, mix_ref,
                  acc, xhs, dn, n2s, invs, *, tile):
    f = pl.program_id(0)
    last = pl.num_programs(0) - 1
    docs, rows, d = x_ref.shape
    groups, w = att_ref.shape[0], att_ref.shape[3]
    tiles = [(i, r) for i in range(docs) for r in range(0, rows, tile)]

    @pl.when(f == 0)
    def _():
        for i, r in tiles:
            at = slice(i * rows + r, i * rows + r + tile)
            res = x_ref[i, r:r + tile, :].astype(F32)
            for g in range(groups):
                res = res + dot(att_ref[g, i, r:r + tile, :], wo_ref[g * w:(g + 1) * w, :])
            acc[at, :] = res
            xh, inv = normalise(res)
            xhs[at, :] = xh
            invs[at, :] = jnp.broadcast_to(inv, (tile, 128))
            n2s[at, :] = (xh * gain_ref[...]).astype(BF)
            dn[at, :] = jnp.zeros((tile, d), F32)

    def first(i, r):
        at = slice(i * rows + r, i * rows + r + tile)
        return dot(n2s[at, :], up_ref[...]), dot(cot_ref[i, r:r + tile, :], down_ref[...], NT)

    ahead = first(*tiles[0])
    for t, (i, r) in enumerate(tiles):
        u, g = ahead
        if t + 1 < len(tiles):
            ahead = first(*tiles[t + 1])
        at = slice(i * rows + r, i * rows + r + tile)
        act, slope = gelu_parts(u)
        pg = (slope * g).astype(BF)
        acc[at, :] += dot(act.astype(BF), down_ref[...])
        dn[at, :] += dot(pg, up_ref[...], NT)

    @pl.when(f == last)
    def _():
        for i, r in tiles:
            at = slice(i * rows + r, i * rows + r + tile)
            out_ref[i, r:r + tile, :] = acc[at, :].astype(BF)
            rg = cot_ref[i, r:r + tile, :].astype(F32) + norm_back(xhs[at, :], invs[at, :1], gain_ref[...], dn[at, :])
            res_ref[i, r:r + tile, :] = rg
            rgb = rg.astype(BF)
            for g in range(groups):
                mix_ref[g, i, r:r + tile, :] = dot(rgb, wo_ref[g * w:(g + 1) * w, :], NT).astype(BF)

def middle(x, att, cot, gain, wo, up, down, chunk=512, tile=512):
    docs, rows, d = x.shape
    groups, _, _, w = att.shape
    ff = up.shape[1]
    tile = min(tile, rows)
    full = lambda a: pl.BlockSpec(a.shape, lambda i: (0,) * a.ndim, pipeline_mode=pl.Buffered(1))
    outs = [jax.ShapeDtypeStruct((docs, rows, d), BF), jax.ShapeDtypeStruct((docs, rows, d), F32),
            jax.ShapeDtypeStruct((groups, docs, rows, w), BF)]
    n = docs * rows
    return pl.pallas_call(
        functools.partial(middle_kernel, tile=tile),
        grid=(ff // chunk,),
        in_specs=[full(x), full(att), full(cot), full(gain), full(wo),
                  pl.BlockSpec((d, chunk), lambda i: (0, i)), pl.BlockSpec((chunk, d), lambda i: (i, 0))],
        out_specs=[full(o) for o in outs],
        out_shape=outs,
        scratch_shapes=[pltpu.VMEM((n, d), F32), pltpu.VMEM((n, d), F32), pltpu.VMEM((n, d), F32),
                        pltpu.VMEM((n, d), BF), pltpu.VMEM((n, 128), F32)],
        compiler_params=pltpu.CompilerParams(vmem_limit_bytes=63 << 20),
        name="feed_forward",
    )(x, att, cot, gain, wo, up, down)

def final_kernel(x_ref, gain_ref, dq_ref, dk_ref, dv_ref, res_ref, low_ref, w_ref, down_ref, up_ref,
                 out_ref, gdown_ref, gup_ref):
    i = pl.program_id(0)
    groups, w = dq_ref.shape[0], dq_ref.shape[3]
    xh, inv = normalise(x_ref[0].astype(F32))
    n1 = (xh * gain_ref[...]).astype(BF)

    @pl.when(i == 0)
    def _():
        gdown_ref[...] = jnp.zeros_like(gdown_ref)
        gup_ref[...] = jnp.zeros_like(gup_ref)

    low = low_ref[0]
    fg = lg = None
    for g in range(groups):
        for part, ref in enumerate((dq_ref, dk_ref, dv_ref)):
            cols = slice((3 * g + part) * w, (3 * g + part + 1) * w)
            piece = ref[g, 0]
            y = dot(piece, w_ref[:, cols], NT)
            fg = y if fg is None else fg + y
            if part != 1:
                y = dot(piece, up_ref[:, cols], NT)
                lg = y if lg is None else lg + y
                gup_ref[:, cols] += dot(low, piece, TN)
    lgb = lg.astype(BF)
    fg = fg + dot(lgb, down_ref[...], NT)
    gdown_ref[...] += dot(lgb, n1, TN)
    out_ref[0] = (res_ref[0] + norm_back(xh, inv, gain_ref[...], fg)).astype(BF)

def final(x, gain, dq, dk, dv, res, low, w, down, up):
    docs, rows, d = x.shape
    groups, _, _, wid = dq.shape
    full = lambda a: pl.BlockSpec(a.shape, lambda i: (0,) * a.ndim)
    row = pl.BlockSpec((1, rows, d), lambda i: (i, 0, 0))
    part = pl.BlockSpec((groups, 1, rows, wid), lambda i: (0, i, 0, 0))
    outs = [jax.ShapeDtypeStruct((docs, rows, d), BF), jax.ShapeDtypeStruct((128, d), F32),
            jax.ShapeDtypeStruct((128, w.shape[1]), F32)]
    return pl.pallas_call(
        final_kernel,
        grid=(docs,),
        in_specs=[row, full(gain), part, part, part, row, pl.BlockSpec((1, rows, 128), lambda i: (i, 0, 0)),
                  full(w), full(down), full(up)],
        out_specs=[row, full(outs[1]), full(outs[2])],
        out_shape=outs,
        compiler_params=pltpu.CompilerParams(vmem_limit_bytes=60 << 20),
        name="projection_gradients",
    )(x, gain, dq, dk, dv, res, low, w, down, up)

ADAPTER_SCALE = 8.0
AXES = ("batch", "seq")


def swapped(b, s):
    return (b & ~1) | (s & 1), (s & ~1) | (b & 1)


def local(
    nb, ns,
    tokens, cotangent, layout, attention_norm_gain, feedforward_norm_gain,
    query_weight, key_weight, value_weight, attention_output_weight, up_weight, down_weight,
    query_down_adapter, query_up_adapter, value_down_adapter, value_up_adapter,
):
    docs, rows, d = tokens.shape
    size = rows * ns // layout.shape[0]
    w = d // ns
    swap = []
    for b in range(nb):
        for s in range(ns):
            b2, s2 = swapped(b, s)
            swap.append((b * ns + s, b2 * ns + s2))
    seq_index = (lax.axis_index("seq") & ~1) | (lax.axis_index("batch") & 1)

    def cross(a):
        return lax.ppermute(a, AXES, swap)

    def peer_swap(a, r):
        perm = []
        for b in range(nb):
            for s in range(ns):
                b2, s2 = swapped(b, s)
                b3, s3 = swapped(b2, s2 ^ r)
                perm.append((b * ns + s, b3 * ns + s3))
        return lax.ppermute(a, AXES, perm)

    def exchange(a):
        out = lax.dynamic_update_index_in_dim(
            jnp.zeros_like(a), lax.dynamic_index_in_dim(a, seq_index, 0), seq_index, 0)
        for r in range(1, ns):
            got = peer_swap(lax.dynamic_index_in_dim(a, seq_index ^ r, 0), r)
            out = lax.dynamic_update_index_in_dim(out, got, seq_index ^ r, 0)
        return out

    def interleave(q, k, v):
        cols = []
        for g in range(ns):
            for a in (q, k, v):
                cols.append(a[:, g * w:(g + 1) * w])
        return jnp.concatenate(cols, axis=1)

    x = cross(tokens)
    cot = cross(cotangent)
    w_qkv = lax.all_gather(interleave(query_weight, key_weight, value_weight), "batch", axis=0, tiled=True)
    w_o = lax.all_gather(attention_output_weight, "batch", axis=0, tiled=True)
    w_up = lax.all_gather(up_weight, "batch", axis=0, tiled=True)
    w_down = lax.all_gather(down_weight, "batch", axis=0, tiled=True)
    rank = query_up_adapter.shape[0]
    down8 = jnp.pad(jnp.concatenate([query_down_adapter, value_down_adapter], axis=1), ((0, 0), (0, 128 - 2 * rank)))
    none = jnp.zeros_like(query_up_adapter)
    up8 = jnp.pad(
        ADAPTER_SCALE * jnp.concatenate(
            [interleave(query_up_adapter, none, none), interleave(none, none, value_up_adapter)], axis=0),
        ((0, 128 - 2 * rank), (0, 0))).astype(BF)
    where = jnp.argsort(layout).astype(jnp.int32)
    gain1 = attention_norm_gain[None]
    gain2 = feedforward_norm_gain[None]

    qkv, low = project(x, gain1, w_qkv, down8, up8, ns)
    qkv = exchange(qkv)
    att, lse = att_fwd(where, qkv, size)
    layer_out, res, mix = middle(x, exchange(att), cot, gain2, w_o, w_up, w_down)
    layer_out = cross(layer_out)
    dq, dk, dv = att_bwd(where, qkv, att, exchange(mix), lse, size)
    dq, dk, dv = exchange(dq), exchange(dk), exchange(dv)
    input_grad, gdown, gup = final(x, gain1, dq, dk, dv, res, low, w_qkv, down8, up8)
    input_grad = cross(input_grad)
    gup = gup[:2 * rank].reshape(2 * rank, ns, 3, w)
    sums = jnp.concatenate([
        gdown[:rank], gdown[rank:2 * rank],
        ADAPTER_SCALE * gup[:rank, :, 0].reshape(rank, d),
        ADAPTER_SCALE * gup[rank:, :, 2].reshape(rank, d)], axis=0)
    sums = lax.psum(sums, AXES)
    return (layer_out, input_grad, sums[:rank].T, sums[2 * rank:3 * rank], sums[rank:2 * rank].T, sums[3 * rank:])


def solution(mesh):
    spec = P("batch", "seq", None)
    weight = P("batch", None)
    return jax.shard_map(
        functools.partial(local, mesh.shape["batch"], mesh.shape["seq"]),
        mesh=mesh,
        in_specs=(spec, spec, P(), P(), P()) + (weight,) * 6 + (P(),) * 4,
        out_specs=(spec, spec, P(), P(), P(), P()),
        check_vma=False,
    )
```

time: 1380 us -> 615 us (0.45)
  matrix products: 562 us -> 0 us
  waiting for transfers between devices: 516 us -> 296 us
  Pallas kernels: 0 us -> 210 us
  other arithmetic: 100 us -> 2.16 us
  local copies, waits for them, and re-layouts: 142 us -> 52.8 us
  starting transfers between devices: 0.9 us -> 32.8 us
  loops' own time: 22.9 us -> 0 us
    dot_general x90 -> x0, matrix products: 562 us -> none  [the longest x27 113 us: contracted_against(): lax.dot_general(left_op, right_op, (((1,), (1,)), ((), ())), preferred_el...]
    all_gather x18 -> x4, waiting for transfers between devices: 362 us -> 113 us  [the longest x1 75.2 us: local(): w_up = lax.all_gather(up_weight, 'batch', axis=0, tiled=True)]
    pallas_call x0 -> x5, Pallas kernels: none -> 210 us  [the longest x1 85.6 us: middle(): pl.pallas_call(functools.partial(middle_kernel, tile=tile), grid=(ff // c...]
    reduce_sum x34 -> x0, other arithmetic: 66.5 us -> none  [the longest x3 43 us: key_fold(): new_sum = jnp.sum(weights_now, axis=-1)]
    dynamic_slice x24 -> x6, local copies, waits for them, and re-layouts: 59.6 us -> 6.71 us  [exchange(): got = peer_swap(lax.dynamic_index_in_dim(a, seq_index ^ r, 0), r)]
    ppermute x0 -> x10, waiting for transfers between devices: none -> 44.5 us  [the longest x4 34.1 us: cross(): return lax.ppermute(a, AXES, swap)]
    ppermute x0 -> x10, starting transfers between devices: none -> 32.6 us  [the longest x6 19.3 us: peer_swap(): return lax.ppermute(a, AXES, perm)]
    all_gather x6 -> x0, local copies, waits for them, and re-layouts: 23.6 us -> none  [the longest x3 11.8 us: forward_one(): lax.all_gather(value_rows, 'seq', axis=0, tiled=True)]
  transfers between devices with their start and end apart: 25 -> 15, of which waited for: 16 -> 9; matrix products, arithmetic and copies ran while one was open for 44% -> 5% of each run, Pallas kernels for 0% -> 13%
where the time goes in v1:
time: 615 us; the launch traced here: 608 us
  waiting for transfers between devices  296 us (48%)
  Pallas kernels  210 us (34%)
  local copies, waits for them, and re-layouts  52.8 us (9%)
  starting transfers between devices  32.8 us (5%)
  between operations  14.5 us (2%)
    psum x1, waiting for transfers between devices, local(): sums = lax.psum(sums, AXES)  137 us
    pallas_call x1, Pallas kernels, middle(): pl.pallas_call(functools.partial(middle_kernel, tile=tile), grid=(ff // c...  85.6 us
    all_gather x1, waiting for transfers between devices, local(): w_up = lax.all_gather(up_weight, 'batch', axis=0, tiled=True)  75.2 us
    pallas_call x1, Pallas kernels, att_bwd(): pl.pallas_call(functools.partial(att_bwd_kernel, blocks=blocks, size=size...  47.4 us
    ppermute x4, waiting for transfers between devices, cross(): return lax.ppermute(a, AXES, swap)  34.1 us
    pallas_call x1, Pallas kernels, att_fwd(): pl.pallas_call(functools.partial(att_fwd_kernel, blocks=blocks, size=size...  31 us
    pallas_call x1, Pallas kernels, final(): pl.pallas_call(final_kernel, grid=(docs,), in_specs=[row, full(gain), par...  25 us
    unnamed x33, local copies, waits for them, and re-layouts  24.1 us
  transfers between devices with their start and end apart: 15, of which 9 were waited for; matrix products, arithmetic and copies ran while one was open for 5% of the time, Pallas kernels for 13%

profile of v1, /device:TPU:1, one launch (start us, length us, event | category | flops | bytes accessed | tf_op | source)
XLA Modules:
  0.0 608.2 jit_solution(14726759161643513573)
XLA Ops:
  7.2 0.8 slice_dynamic-update-slice_fusion.5
  8.1 0.8 slice_dynamic-update-slice_fusion.4
  8.9 0.8 slice_dynamic-update-slice_fusion.3
  9.7 0.8 slice_dynamic-update-slice_fusion.2
  10.6 0.8 slice_dynamic-update-slice_fusion.1
  11.4 0.8 slice_dynamic-update-slice_fusion
  12.3 0.7 copy-done.11
  13.1 0.7 all-gather.7.cloned.1.call-update
  13.8 0.7 all-gather.11.cloned.1.call-update
  14.6 0.5 all-gather.9.cloned.1.call-update
  15.2 4.5 collective-permute-start
  19.7 0.7 pad_maximum_fusion.1
  20.6 0.7 fusion.1
  21.4 1.0 pad.9.up_ref
  22.4 0.8 pad.8.down_ref
  23.2 32.1 %collective-permute-done.x_ref = bf16[3,512,1024]{2,1,0:T(8,128)(2,1)S(1)} collective-permute-done((bf16[3,512,1024]{2,1,0:T(8,128)(2,1)}, bf16[3,512,1024]{2,1,0:T(8,128)(2,1)S(1)}, u32[]{:S(2)}, u32[]{:S(2)}) %collective-permute-start) | collective-permute-done | bytes 3145760 | tf_op jit(solution)/shard_map/ppermute | solution.py:368
  55.2 22.3 %all-gather.5.cloned.1.call-done.w_ref = bf16[1024,3072]{1,0:T(8,128)(2,1)} async-done(((bf16[64,3072]{1,0:T(8,128)(2,1)}), bf16[1024,3072]{1,0:T(8,128)(2,1)}) %all-gather.5.cloned.1.call-update) | async-done | bytes 6291472 | tf_op jit(solution)/shard_map/all_gather | solution.py:396
  77.6 20.7 %projections.1 = (bf16[2,3,512,1536]{3,2,1,0:T(8,128)(2,1)}, bf16[3,512,128]{2,1,0:T(8,128)(2,1)}) custom-call(bf16[3,512,1024]{2,1,0:T(8,128)(2,1)} %copy-done, f32[1,1024]{1,0:T(1,128)} %bitcast.12, bf16[1024,3072]{1,0:T(8,128)(2,1)} %all-gather.5.cloned.1.call-done.w_ref, bf16[1024,128]{1,0:T(8,128)(2,1)} %pad.8.down_ref, bf16[128,3072]{1,0:T(8,128)(2,1)} %pad.9.up_ref), custom_call_target="tpu_custom_call" | custom-call | tf_op jit(solution)/shard_map/projections/pallas_call | solution.py:213
  98.3 5.6 broadcast_in_dim.9
  103.9 1.5 copy-done.6
  105.4 4.2 constant_dynamic-slice_fusion.5
  109.9 3.2 collective-permute-start.3
  113.2 0.8 sort.17
  113.9 4.2 collective-permute-done.1
  118.1 4.8 constant_dynamic-update-slice_fusion.4.q_ref.k_ref.v_ref
  122.9 31.0 %attention_forward.1 = (bf16[2,3,512,512]{3,2,1,0:T(8,128)(2,1)}, f32[3,4,2,1024]{3,2,1,0:T(2,128)}) custom-call(s32[4]{0:T(128)} %get-tuple-element.20.where, bf16[2,3,512,1536]{3,2,1,0:T(8,128)(2,1)} %constant_dynamic-update-slice_fusion.4.q_ref.k_ref.v_ref, bf16[2,3,512,1536]{3,2,1,0:T(8,128)(2,1)} %constant_dynamic-update-slice_fusion.4.q_ref.k_ref.v_ref, ...), custom_call_target="tpu_custom_call" | custom-call | tf_op jit(solution)/shard_map/attention_forward/pallas_call | solution.py:80
  153.8 2.0 broadcast.16.clone
  155.8 1.3 copy-done.4
  157.1 1.3 constant_dynamic-slice_fusion.3
  158.4 17.7 %collective-permute-start.2 = (bf16[1,3,512,512]{3,2,1,0:T(8,128)(2,1)S(1)}, bf16[1,3,512,512]{3,2,1,0:T(8,128)(2,1)S(1)}, u32[]{:S(2)}, u32[]{:S(2)}) collective-permute-start(bf16[1,3,512,512]{3,2,1,0:T(8,128)(2,1)S(1)} %get-tuple-element.44), channel_id=1, source_target_pairs={{0,2},{1,3},{2,0},{3,1},{4,6},{5,7},{6,4},{7,5},{8,10},{9,11},{10,... | collective-permute-start | bytes 4718600 | tf_op jit(solution)/shard_map/ppermute | solution.py:377
  176.1 3.0 collective-permute-done.2
  179.2 1.2 constant_dynamic-update-slice_fusion.3.att_ref
  180.4 15.2 %all-gather.11.cloned.1.call-done.down_ref = bf16[4096,1024]{1,0:T(8,128)(2,1)} async-done(((bf16[256,1024]{1,0:T(8,128)(2,1)}), bf16[4096,1024]{1,0:T(8,128)(2,1)}) %all-gather.11.cloned.1.call-update) | async-done | bytes 8388624 | tf_op jit(solution)/shard_map/all_gather | solution.py:399
  195.6 75.2 %all-gather.9.cloned.1.call-done.up_ref = bf16[1024,4096]{1,0:T(8,128)(2,1)} async-done(((bf16[64,4096]{1,0:T(8,128)(2,1)}), bf16[1024,4096]{1,0:T(8,128)(2,1)}) %all-gather.9.cloned.1.call-update) | async-done | bytes 8388624 | tf_op jit(solution)/shard_map/all_gather | solution.py:398
  270.8 85.6 %feed_forward.1 = (bf16[3,512,1024]{2,1,0:T(8,128)(2,1)}, f32[3,512,1024]{2,1,0:T(8,128)}, bf16[2,3,512,512]{3,2,1,0:T(8,128)(2,1)}) custom-call(bf16[3,512,1024]{2,1,0:T(8,128)(2,1)} %copy-done, bf16[2,3,512,512]{3,2,1,0:T(8,128)(2,1)} %constant_dynamic-update-slice_fusion.3.att_ref, bf16[3,512,1024]{2,1,0:T(8,128)(2,1)} %collective-permute-done.3.cot_ref, ...), custom_call_target="tpu_custom_call" | custom-call | tf_op jit(solution)/shard_map/feed_forward/pallas_call | solution.py:282
  356.8 1.6 copy-done.9
  358.4 0.3 constant_dynamic-slice_fusion.2
  358.7 0.3 collective-permute-start.5
  359.0 3.1 collective-permute-done.5
  362.3 1.7 copy-done.5
  364.0 47.4 %attention_backward.1 = (bf16[2,3,512,512]{3,2,1,0:T(8,128)(2,1)}, bf16[2,3,512,512]{3,2,1,0:T(8,128)(2,1)}, bf16[2,3,512,512]{3,2,1,0:T(8,128)(2,1)}) custom-call(s32[4]{0:T(128)} %get-tuple-element.20.where, bf16[2,3,512,1536]{3,2,1,0:T(8,128)(2,1)} %constant_dynamic-update-slice_fusion.4.q_ref.k_ref.v_ref, ...), custom_call_target="tpu_custom_call" | custom-call | tf_op jit(solution)/shard_map/attention_backward/pallas_call | solution.py:162
  411.6 1.6 copy-done.10
  413.2 0.3 constant_dynamic-slice_fusion.1
  413.5 0.3 collective-permute-start.8
  414.1 1.3 copy-done.8
  415.4 0.3 constant_dynamic-slice_fusion.4
  415.7 0.3 collective-permute-start.7
  416.3 1.3 copy-done.7
  417.6 0.3 constant_dynamic-slice_fusion
  417.9 0.3 collective-permute-start.6
  418.2 3.2 collective-permute-start.4
  422.0 1.3 copy-done.2
  423.3 1.0 copy-done.3
  424.4 1.0 copy-done.1
  425.4 25.0 %projection_gradients.1 = (bf16[3,512,1024]{2,1,0:T(8,128)(2,1)}, f32[128,1024]{1,0:T(8,128)}, f32[128,3072]{1,0:T(8,128)}) custom-call(bf16[3,512,1024]{2,1,0:T(8,128)(2,1)} %copy-done, f32[1,1024]{1,0:T(1,128)} %bitcast.13, bf16[2,3,512,512]{3,2,1,0:T(8,128)(2,1)} %copy-done.1, bf16[2,3,512,512]{3,2,1,0:T(8,128)(2,1)} %copy-done.3, ...), custom_call_target="tpu_custom_call" | custom-call | tf_op jit(solution)/shard_map/projection_gradients/pallas_call | solution.py:332
  450.4 2.3 collective-permute-start.9
  452.7 0.9 slice.67
  453.6 0.8 slice.66
  454.4 0.6 pad_maximum_fusion
  455.0 2.1 collective-permute-done.4
  457.1 137.1 %all-reduce.4.cloned.1.call-done = f32[16,1024]{1,0:T(8,128)} async-done(((f32[16,1024]{1,0:T(8,128)}), f32[16,1024]{1,0:T(8,128)}) %all-reduce.4.cloned.1.call-update) | async-done | bytes 65552 | tf_op jit(solution)/shard_map/psum | solution.py:425
  594.2 1.5 fusion
  595.7 3.9 copy.46
  599.6 1.7 copy.47
  (42 shorter events, 2.4 us)
Async XLA Ops:
  7.2 70.4 %all-gather.5.cloned.1.call-start = ((), (), s32[]{:S(2)}) async-start(), calls=%async_computation | async-start | bytes 6684672 | tf_op jit(solution)/shard_map/all_gather | solution.py:396
  12.3 0.7 copy-start.11
  13.1 167.4 %all-gather.7.cloned.1.call-start = ((), (), s32[]{:S(2)}) async-start(), calls=%async_computation.1 | async-start | bytes 2228224 | tf_op jit(solution)/shard_map/all_gather | solution.py:397
  13.8 181.8 %all-gather.11.cloned.1.call-start = ((), (), s32[]{:S(2)}) async-start(), calls=%async_computation.3 | async-start | bytes 8912896 | tf_op jit(solution)/shard_map/all_gather | solution.py:399
  14.5 256.3 %all-gather.9.cloned.1.call-start = ((), (), s32[]{:S(2)}) async-start(), calls=%async_computation.2 | async-start | bytes 8912896 | tf_op jit(solution)/shard_map/all_gather | solution.py:398
  15.1 579.1 %all-reduce.4.cloned.1.call-start = ((), (), s32[]{:S(2)}) async-start(), calls=%async_computation.4 | async-start | bytes 131072 | tf_op jit(solution)/shard_map/psum | solution.py:425
  15.2 40.1 %collective-permute-start = (bf16[3,512,1024]{2,1,0:T(8,128)(2,1)}, bf16[3,512,1024]{2,1,0:T(8,128)(2,1)S(1)}, u32[]{:S(2)}, u32[]{:S(2)}) collective-permute-start(bf16[3,512,1024]{2,1,0:T(8,128)(2,1)} %param.15), channel_id=1, source_target_pairs={{0,0},{1,2},{2,1},{3,3},{4,4},{5,6},{6,5},{7,7},{8,8},{9,10},{10,9... | collective-permute-start | bytes 9437192 | tf_op jit(solution)/shard_map/ppermute | solution.py:368
  55.2 22.3 %copy-start = (bf16[3,512,1024]{2,1,0:T(8,128)(2,1)}, bf16[3,512,1024]{2,1,0:T(8,128)(2,1)S(1)}, u32[]{:S(2)}) copy-start(bf16[3,512,1024]{2,1,0:T(8,128)(2,1)S(1)} %collective-permute-done.x_ref) | copy-start | bytes 9437188
  98.3 7.1 %copy-start.6 = (bf16[2,3,512,1536]{3,2,1,0:T(8,128)(2,1)S(1)}, bf16[2,3,512,1536]{3,2,1,0:T(8,128)(2,1)}, u32[]{:S(2)}) copy-start(bf16[2,3,512,1536]{3,2,1,0:T(8,128)(2,1)} %get-tuple-element.21) | copy-start | bytes 28311556
  105.4 7.7 %copy-start.12 = (s32[4]{0:T(128)S(1)}, s32[4]{0:T(128)}, u32[]{:S(2)}) copy-start(s32[4]{0:T(128)} %param.17) | copy-start | bytes 52
  109.6 8.4 %collective-permute-start.1 = (bf16[1,3,512,1536]{3,2,1,0:T(8,128)(2,1)}, bf16[1,3,512,1536]{3,2,1,0:T(8,128)(2,1)}, u32[]{:S(2)}, u32[]{:S(2)}) collective-permute-start(bf16[1,3,512,1536]{3,2,1,0:T(8,128)(2,1)} %get-tuple-element.34), channel_id=1, source_target_pairs={{0,2},{1,3},{2,0},{3,1},{4,6},{5,7},{6,4},{7,5},{8,10},{9,11},{10,... | collective-permute-start | bytes 14155784 | tf_op jit(solution)/shard_map/ppermute | solution.py:377
  109.9 70.5 %collective-permute-start.3 = (bf16[3,512,1024]{2,1,0:T(8,128)(2,1)}, bf16[3,512,1024]{2,1,0:T(8,128)(2,1)}, u32[]{:S(2)}, u32[]{:S(2)}) collective-permute-start(bf16[3,512,1024]{2,1,0:T(8,128)(2,1)} %param.16), channel_id=1, source_target_pairs={{0,0},{1,2},{2,1},{3,3},{4,4},{5,6},{6,5},{7,7},{8,8},{9,10},{10,9... | collective-permute-start | bytes 9437192 | tf_op jit(solution)/shard_map/ppermute | solution.py:368
  153.8 3.3 copy-start.4
  158.4 20.7 %collective-permute-start.2 = (bf16[1,3,512,512]{3,2,1,0:T(8,128)(2,1)S(1)}, bf16[1,3,512,512]{3,2,1,0:T(8,128)(2,1)S(1)}, u32[]{:S(2)}, u32[]{:S(2)}) collective-permute-start(bf16[1,3,512,512]{3,2,1,0:T(8,128)(2,1)S(1)} %get-tuple-element.44), channel_id=1, source_target_pairs={{0,2},{1,3},{2,0},{3,1},{4,6},{5,7},{6,4},{7,5},{8,10},{9,11},{10,... | collective-permute-start | bytes 4718600 | tf_op jit(solution)/shard_map/ppermute | solution.py:377
  356.5 1.9 copy-start.9
  358.7 3.5 collective-permute-start.5
  362.3 1.7 copy-start.5
  411.3 1.9 copy-start.10
  413.5 1.9 copy-start.8
  413.5 7.9 %collective-permute-start.8 = (bf16[1,3,512,512]{3,2,1,0:T(8,128)(2,1)S(1)}, bf16[1,3,512,512]{3,2,1,0:T(8,128)(2,1)S(1)}, u32[]{:S(2)}, u32[]{:S(2)}) collective-permute-start(bf16[1,3,512,512]{3,2,1,0:T(8,128)(2,1)S(1)} %get-tuple-element.36), channel_id=1, source_target_pairs={{0,2},{1,3},{2,0},{3,1},{4,6},{5,7},{6,4},{7,5},{8,10},{9,11},{10,... | collective-permute-start | bytes 4718600 | tf_op jit(solution)/shard_map/ppermute | solution.py:377
  415.7 1.9 copy-start.7
  415.7 5.9 collective-permute-start.7
  417.9 3.9 collective-permute-start.6
  418.2 38.9 %collective-permute-start.4 = (bf16[3,512,1024]{2,1,0:T(8,128)(2,1)}, bf16[3,512,1024]{2,1,0:T(8,128)(2,1)}, u32[]{:S(2)}, u32[]{:S(2)}) collective-permute-start(bf16[3,512,1024]{2,1,0:T(8,128)(2,1)} %get-tuple-element.23), channel_id=1, source_target_pairs={{0,0},{1,2},{2,1},{3,3},{4,4},{5,6},{6,5},{7,7},{8,8},{9,10},{10,9... | collective-permute-start | bytes 9437192 | tf_op jit(solution)/shard_map/ppermute | solution.py:368
  421.6 1.7 copy-start.2
  421.8 2.5 copy-start.3
  423.3 2.0 copy-start.1
  450.4 145.3 %collective-permute-start.9 = (bf16[3,512,1024]{2,1,0:T(8,128)(2,1)}, bf16[3,512,1024]{2,1,0:T(8,128)(2,1)S(1)}, u32[]{:S(2)}, u32[]{:S(2)}) collective-permute-start(bf16[3,512,1024]{2,1,0:T(8,128)(2,1)} %get-tuple-element.31), channel_id=1, source_target_pairs={{0,0},{1,2},{2,1},{3,3},{4,4},{5,6},{6,5},{7,7},{8,8},{9,10},{10,9... | collective-permute-start | bytes 9437192 | tf_op jit(solution)/shard_map/ppermute | solution.py:368
Sparse Core Ops, SparseCore 0:
  13.2 64.3 all-gather.4
  79.7 39.9 all-gather.6
  121.9 73.6 all-gather.10
  197.6 73.1 all-gather.8
  455.2 139.0 all-reduce.3
